TPU v7x, 256 devices: a whole 4x4x8 slice. The times are simulated.
256 devices in a mesh: lvl: 32 (over z, x), blk: 8 (over y, core).
Axes of the slice: x: 4, y: 4, z: 8, core: 2. Of those that a mesh axis runs over, the one named last changes fastest.
Arguments:
- right_sides: bfloat16 [8, 131072, 256], P('blk', 'lvl'), may hold values from -6 to 6
- row_vectors: bfloat16 [131072, 256], P('lvl'), may hold values from -6 to 6
- leaf_basis_in: bfloat16 [8, 1024, 128, 64], P('blk', 'lvl'), may hold values from -0.5 to 0.5
- leaf_basis_out: bfloat16 [8, 1024, 128, 64], P('blk', 'lvl'), may hold values from -0.75 to 0.75
- transfers: bfloat16 [8, 10, 1024, 2, 64, 64], P('blk', None, 'lvl'), may hold values from -0.625 to 0.625
- tile_ranks: int32 [8, 11, 1024], P('blk', None, 'lvl'), may hold values from 32 to 64, as said below
Outputs:
- row_result: bfloat16 [131072, 256], P(('lvl', 'blk'))
- column_result: bfloat16 [8, 131072, 256], P('blk', 'lvl')
Inputs may be any that keep to these rules, and one draw needn't show every extreme that they name: `tile_ranks`: every entry is 32 or 64, and both occur.
All inputs are finite; a program needn't handle non-finite values.
Results may differ from a plain program's by a relative error of at most 0.027.
Values may be sent and summed in bfloat16 or wider, within the bound.
A program may use at most 128 MiB of HBM per device.

v0:
```python
import jax
import jax.numpy as jnp
from jax import lax
from jax.sharding import PartitionSpec as P

LEVELS = 10


def apply_mask(values, rank_table):
    inside = (
        lax.broadcasted_iota(jnp.int32, (1, 1, values.shape[2], 1), 2)
        < rank_table[:, :, None, None]
    )
    return jnp.where(inside, values, jnp.zeros_like(values))


def forward_low(right_block, basis_in, tiles_all, ranks_all, owners):
    local_leaves = basis_in.shape[0]
    rank_width = basis_in.shape[2]
    rhs_count = right_block.shape[1]
    leaf_rows = right_block.reshape(local_leaves, basis_in.shape[1], rhs_count)
    coefficients = jnp.einsum(
        "nlr,nlk->nrk", basis_in, leaf_rows, preferred_element_type=jnp.float32
    )[:, None]
    coefficients = apply_mask(coefficients, ranks_all[0].reshape(local_leaves, 1)).astype(
        jnp.bfloat16
    )
    for height in range(1, LEVELS // 2 + 1):
        span_rows = 2**height
        span_cols = 2 ** (LEVELS - height) // owners
        level_tiles = tiles_all[height - 1].reshape(
            span_cols, span_rows // 2, 2, 2, rank_width, rank_width
        )
        before = coefficients.reshape(span_cols, 2, span_rows // 2, rank_width, rhs_count)
        updated = jnp.einsum(
            "jhbcrs,jchsk->jhbrk", level_tiles, before, preferred_element_type=jnp.float32
        )
        updated = updated.reshape(span_cols, span_rows, rank_width, rhs_count)
        coefficients = apply_mask(updated, ranks_all[height].reshape(span_cols, span_rows)).astype(
            jnp.bfloat16
        )
    return coefficients


def forward_high(coefficients, tiles_all, ranks_all, owners):
    rank_width = coefficients.shape[2]
    rhs_count = coefficients.shape[3]
    for height in range(LEVELS // 2 + 1, LEVELS + 1):
        span_rows = 2**height // owners
        span_cols = 2 ** (LEVELS - height)
        level_tiles = tiles_all[height - 1].reshape(
            span_rows // 2, 2, span_cols, 2, rank_width, rank_width
        )
        before = coefficients.reshape(span_cols, 2, span_rows // 2, rank_width, rhs_count)
        updated = jnp.einsum(
            "hbjcrs,jchsk->jhbrk", level_tiles, before, preferred_element_type=jnp.float32
        )
        updated = updated.reshape(span_cols, span_rows, rank_width, rhs_count)
        rank_table = ranks_all[height].reshape(span_rows, span_cols).T
        coefficients = apply_mask(updated, rank_table).astype(jnp.bfloat16)
    return coefficients


def adjoint_high(row_block, basis_out, tiles_all, ranks_all, owners):
    local_leaves = basis_out.shape[0]
    rank_width = basis_out.shape[2]
    rhs_count = row_block.shape[1]
    leaf_rows = row_block.reshape(local_leaves, basis_out.shape[1], rhs_count)
    adjoint = jnp.einsum("nlr,nlk->nrk", basis_out, leaf_rows, preferred_element_type=jnp.float32)[
        :, None
    ]
    adjoint = apply_mask(adjoint, ranks_all[LEVELS].reshape(local_leaves, 1)).astype(jnp.bfloat16)
    for height in range(LEVELS, LEVELS // 2, -1):
        span_rows = 2**height // owners
        span_cols = 2 ** (LEVELS - height)
        level_tiles = tiles_all[height - 1].reshape(
            span_rows // 2, 2, span_cols, 2, rank_width, rank_width
        )
        current = adjoint.reshape(span_rows // 2, 2, span_cols, rank_width, rhs_count)
        updated = jnp.einsum(
            "hbjcrs,hbjrk->hjcsk", level_tiles, current, preferred_element_type=jnp.float32
        )
        updated = updated.reshape(span_rows // 2, 2 * span_cols, rank_width, rhs_count)
        if height - 1 > LEVELS // 2:
            updated = apply_mask(
                updated, ranks_all[height - 1].reshape(span_rows // 2, 2 * span_cols)
            )
        adjoint = updated.astype(jnp.bfloat16)
    return adjoint


def adjoint_low(adjoint, basis_in, tiles_all, ranks_all, owners):
    rank_width = adjoint.shape[2]
    rhs_count = adjoint.shape[3]
    middle = LEVELS // 2
    rank_table = ranks_all[middle].reshape(2 ** (LEVELS - middle) // owners, 2**middle).T
    adjoint = apply_mask(adjoint, rank_table)
    for height in range(middle, 0, -1):
        span_rows = 2**height
        span_cols = 2 ** (LEVELS - height) // owners
        level_tiles = tiles_all[height - 1].reshape(
            span_cols, span_rows // 2, 2, 2, rank_width, rank_width
        )
        current = adjoint.reshape(span_rows // 2, 2, span_cols, rank_width, rhs_count)
        updated = jnp.einsum(
            "jhbcrs,hbjrk->hjcsk", level_tiles, current, preferred_element_type=jnp.float32
        )
        updated = updated.reshape(span_rows // 2, 2 * span_cols, rank_width, rhs_count)
        rank_table = ranks_all[height - 1].reshape(2 * span_cols, span_rows // 2).T
        adjoint = apply_mask(updated, rank_table).astype(jnp.bfloat16)
    result = jnp.einsum("nlr,nrk->nlk", basis_in, adjoint[0], preferred_element_type=jnp.float32)
    return result.astype(jnp.bfloat16).reshape(-1, rhs_count)


def body(right_sides, row_vectors, leaf_basis_in, leaf_basis_out, transfers, tile_ranks):
    owners = lax.axis_size("lvl")
    groups = lax.axis_size("blk")
    basis_in = leaf_basis_in[0]
    basis_out = leaf_basis_out[0]
    tiles_all = transfers[0]
    ranks_all = tile_ranks[0]
    lower = forward_low(right_sides[0], basis_in, tiles_all, ranks_all, owners)
    mixed = lax.all_to_all(lower, "lvl", split_axis=1, concat_axis=0, tiled=True)
    finest = forward_high(mixed, tiles_all, ranks_all, owners)
    upper = adjoint_high(row_vectors, basis_out, tiles_all, ranks_all, owners)
    crossed = lax.all_to_all(upper, "lvl", split_axis=1, concat_axis=0, tiled=True)
    column_out = adjoint_low(crossed, basis_in, tiles_all, ranks_all, owners)
    width_leaf = basis_out.shape[1]
    rhs_count = finest.shape[3]
    local_leaves = basis_out.shape[0]
    leaf_coefficients = finest[0]
    block_part = jnp.einsum(
        "nlr,nrk->nlk", basis_out, leaf_coefficients, preferred_element_type=jnp.float32
    )
    summed = lax.psum_scatter(
        block_part.astype(jnp.bfloat16)
        .astype(jnp.float32)
        .reshape(local_leaves * width_leaf // groups * lax.axis_size("blk"), rhs_count)
        .astype(jnp.bfloat16),
        "blk",
        scatter_dimension=0,
        tiled=True,
    )
    return (summed, column_out[None])


def solution(mesh):
    return jax.shard_map(
        body,
        mesh=mesh,
        in_specs=(
            P("blk", "lvl", None),
            P("lvl", None),
            P("blk", "lvl", None, None),
            P("blk", "lvl", None, None),
            P("blk", None, "lvl", None, None, None),
            P("blk", None, "lvl"),
        ),
        out_specs=(P(("lvl", "blk"), None), P("blk", "lvl", None)),
        check_vma=False,
    )
```

profile of v0, /device:TPU:10, one launch (start us, length us, event | category | flops | bytes accessed | tf_op | source)
XLA Modules:
  0.0 126.2 jit_solution(17423840229616139291)
XLA Ops:
  7.2 7.9 %fusion.136 = (bf16[1,1,32,2,64,64]{5,4,3,2,1,0:T(8,128)(2,1)}, bf16[1,1,32,2,64,64]{5,4,3,2,1,0:T(8,128)(2,1)}, bf16[1,1,32,2,64,64]{5,4,3,2,1,0:T(8,128)(2,1)}...) fusion(bf16[1,10,32,2,64,64]{5,4,3,2,1,0:T(8,128)(2,1)} %param.10), kind=kLoop, calls=%fused_computation.182 | loop fusion | bytes 10485760 | tf_op jit(solution)/shard_map/slice | solution.py:51
  16.4 1.5 %select_convert_fusion.1 = bf16[32,64,256]{2,1,0:T(8,128)(2,1)S(1)} fusion(bf16[32,128,256]{2,1,0:T(8,128)(2,1)S(1)} %bitcast.334, pred[32,64]{1,0:T(8,128)(4,1)S(1)} %get-tuple-element.39, bf16[1,32,128,64]{2,3,1,0:T(8,128)(2,1)} %param.8), kind=kOutput, calls=%fused_computation.40 | convolution fusion | flops 135266304 | bytes 3672064 | tf_op jit(solution)/shard_map/nlr,nlk->nrk/dot_general | solution.py:22
  20.0 0.9 fusion.23
  21.2 0.9 fusion.26
  22.2 0.9 fusion.29
  23.1 1.3 %fusion.2 = bf16[1,32,64,256]{3,2,0,1:T(8,128)(2,1)} fusion(bf16[16,256,2,64,1]{1,3,4,2,0:T(8,128)(2,1)S(1)} %fusion.29, pred[32,64]{1,0:T(8,128)(4,1)S(1)} %get-tuple-element.40), kind=kLoop, calls=%fused_computation.5 | loop fusion | flops 524288 | bytes 2099200 | tf_op jit(solution)/shard_map/convert_element_type | solution.py:39
  24.5 11.7 %all-to-all-start = ((bf16[1,32,64,256]{3,2,0,1:T(8,128)(2,1)}), bf16[1,32,64,256]{3,2,0,1:T(8,128)(2,1)}, u32[]{:S(2)}, u32[]{:S(2)}) async-start(bf16[1,32,64,256]{3,2,0,1:T(8,128)(2,1)} %fusion.2), calls=%async_computation | async-start | bytes 2097152 | tf_op jit(solution)/shard_map/all_to_all | solution.py:123
  38.5 2.3 %select_convert_fusion = bf16[32,64,256]{2,1,0:T(8,128)(2,1)S(1)} fusion(bf16[32,128,256]{2,1,0:T(8,128)(2,1)} %bitcast.347, pred[32,64]{1,0:T(8,128)(4,1)S(1)} %iota_compare_fusion.19, bf16[1,32,128,64]{2,3,1,0:T(8,128)(2,1)} %param.9), kind=kOutput, calls=%fused_computation.39 | convolution fusion | flops 135266304 | bytes 3672064 | tf_op jit(solution)/shard_map/nlr,nlk->nrk/dot_general | solution.py:69
  42.1 1.1 fusion.44
  43.2 1.1 fusion.47
  44.4 1.9 %fusion.50 = bf16[2,8,256,2,64,1]{2,4,5,3,1,0:T(8,128)(2,1)} fusion(bf16[2,2,8,64,256]{4,3,2,1,0:T(8,128)(2,1)S(1)} %bitcast.388, bf16[2,2,8,2,64,64]{5,4,3,2,1,0:T(8,128)(2,1)S(1)} %bitcast.358, pred[2,2,8,64]{3,1,2,0:T(4,128)(4,1)S(1)} %iota_compare_fusion.2), kind=kOutput, calls=%fused_computation.64 | convolution fusion | flops 134742016 | bytes 2623488 | tf_op jit(solution)/shard_map/hbjcrs,hbjrk->hjcsk/dot_general | solution.py:80
  46.3 18.0 %all-to-all-done = bf16[1,32,64,256]{3,2,0,1:T(8,128)(2,1)} async-done(((bf16[1,32,64,256]{3,2,0,1:T(8,128)(2,1)}), bf16[1,32,64,256]{3,2,0,1:T(8,128)(2,1)}, u32[]{:S(2)}, u32[]{:S(2)}) %all-to-all-start) | async-done | bytes 1048608 | tf_op jit(solution)/shard_map/all_to_all | solution.py:123
  64.3 2.1 %fusion.78 = bf16[16,256,2,64,1]{1,3,4,2,0:T(8,128)(2,1)S(1)} fusion(bf16[16,2,64,256,1]{3,2,1,4,0:T(8,128)(2,1)} %bitcast.65, bf16[2,16,2,64,64]{4,3,2,1,0:T(8,128)(2,1)} %bitcast.340), kind=kOutput, calls=%fused_computation.86 | convolution fusion | flops 134217728 | bytes 2621440 | tf_op jit(solution)/shard_map/hbjcrs,jchsk->jhbrk/dot_general | solution.py:55
  66.4 0.9 fusion.32
  71.5 2.1 %convolution_convert_fusion.1 = bf16[32,256,128]{1,2,0:T(8,128)(2,1)} fusion(bf16[32,64,256]{2,1,0:T(8,128)(2,1)S(1)} %fusion.1, bf16[1,32,128,64]{2,3,1,0:T(8,128)(2,1)S(1)} %copy-done.4), kind=kOutput, calls=%fused_computation.42 | convolution fusion | flops 135266304 | bytes 3670016 | tf_op jit(solution)/shard_map/nlr,nrk->nlk/dot_general | solution.py:132
  73.7 3.3 %bitcast_convert_fusion = bf16[16,256,2,64]{1,3,2,0:T(8,128)(2,1)} fusion(bf16[2,16,64,256]{3,2,1,0:T(8,128)(2,1)} %bitcast.377, bf16[2,16,2,64,64]{4,3,2,1,0:T(8,128)(2,1)} %bitcast.341, pred[2,16,64]{2,0,1:T(4,128)(4,1)S(1)} %iota_compare_fusion.3), kind=kOutput, calls=%fused_computation.6 | convolution fusion | flops 135266304 | bytes 2623488 | tf_op jit(solution)/shard_map/hbjcrs,hbjrk->hjcsk/dot_general | solution.py:80
  77.0 5.6 %all-to-all-start.1 = ((bf16[1,32,64,256]{3,2,0,1:T(8,128)(2,1)}), bf16[1,32,64,256]{3,2,0,1:T(8,128)(2,1)}, u32[]{:S(2)}, u32[]{:S(2)}) async-start(bf16[1,32,64,256]{3,2,0,1:T(8,128)(2,1)} %bitcast.364), calls=%async_computation.2 | async-start | bytes 2097152 | tf_op jit(solution)/shard_map/all_to_all | solution.py:126
  83.9 25.8 %all-to-all-done.1 = bf16[1,32,64,256]{3,2,0,1:T(8,128)(2,1)} async-done(((bf16[1,32,64,256]{3,2,0,1:T(8,128)(2,1)}), bf16[1,32,64,256]{3,2,0,1:T(8,128)(2,1)}, u32[]{:S(2)}, u32[]{:S(2)}) %all-to-all-start.1) | async-done | bytes 1048608 | tf_op jit(solution)/shard_map/all_to_all | solution.py:126
  109.7 2.4 %fusion.66 = bf16[16,256,2,64,1]{1,3,2,4,0:T(8,128)(2,1)S(1)} fusion(bf16[16,2,2,64,64]{4,3,2,1,0:T(8,128)(2,1)} %bitcast.338, bf16[16,2,64,256]{3,2,1,0:T(8,128)(2,1)} %bitcast.136, pred[16,2,64]{2,1,0:T(4,128)(4,1)S(1)} %iota_compare_fusion.4), kind=kOutput, calls=%fused_computation.74 | convolution fusion | flops 134742016 | bytes 2623488 | tf_op jit(solution)/shard_map/jhbcrs,hbjrk->hjcsk/dot_general | solution.py:105
  112.1 1.1 fusion.55
  113.3 1.1 fusion.58
  114.5 1.1 fusion.61
  115.6 1.1 fusion.64
  117.2 2.1 %convolution_convert_fusion = bf16[32,256,128]{1,2,0:T(8,128)(2,1)} fusion(bf16[32,64,256]{2,1,0:T(8,128)(2,1)S(1)} %fusion, bf16[1,32,128,64]{2,3,1,0:T(8,128)(2,1)S(1)} %copy-done.5), kind=kOutput, calls=%fused_computation.41 | convolution fusion | flops 135266304 | bytes 3670016 | tf_op jit(solution)/shard_map/nlr,nrk->nlk/dot_general | solution.py:111
  (104 shorter events, 13.4 us)
Async XLA Ops:
  7.2 9.2 %copy-start = (bf16[1,4096,256]{2,1,0:T(8,128)(2,1)S(1)}, bf16[1,4096,256]{2,1,0:T(8,128)(2,1)}, u32[]{:S(2)}) copy-start(bf16[1,4096,256]{2,1,0:T(8,128)(2,1)} %param.6) | copy-start | bytes 6291460
  7.2 7.9 %copy-start.18 = (s32[1,11,32]{2,0,1:T(1,128)S(1)}, s32[1,11,32]{2,0,1:T(1,128)}, u32[]{:S(2)}) copy-start(s32[1,11,32]{2,0,1:T(1,128)} %param.11) | copy-start | bytes 4228
  17.9 1.2 copy-start.6
  18.4 1.6 %copy-start.8 = (bf16[1,1,32,2,64,64]{5,4,3,2,1,0:T(8,128)(2,1)S(1)}, bf16[1,1,32,2,64,64]{5,4,3,2,1,0:T(8,128)(2,1)}, u32[]{:S(2)}) copy-start(bf16[1,1,32,2,64,64]{5,4,3,2,1,0:T(8,128)(2,1)} %get-tuple-element.17) | copy-start | bytes 1572868
  20.0 1.2 copy-start.10
  20.9 1.3 %copy-start.1 = (bf16[1,1,32,2,64,64]{5,4,3,2,1,0:T(8,128)(2,1)S(1)}, bf16[1,1,32,2,64,64]{5,4,3,2,1,0:T(8,128)(2,1)}, u32[]{:S(2)}) copy-start(bf16[1,1,32,2,64,64]{5,4,3,2,1,0:T(8,128)(2,1)} %get-tuple-element.15) | copy-start | bytes 1572868
  24.5 39.8 %all-to-all-start = ((bf16[1,32,64,256]{3,2,0,1:T(8,128)(2,1)}), bf16[1,32,64,256]{3,2,0,1:T(8,128)(2,1)}, u32[]{:S(2)}, u32[]{:S(2)}) async-start(bf16[1,32,64,256]{3,2,0,1:T(8,128)(2,1)} %fusion.2), calls=%async_computation | async-start | bytes 2097152 | tf_op jit(solution)/shard_map/all_to_all | solution.py:123
  36.2 83.2 %reduce-scatter.2.cloned.1.call-start = ((), (), s32[]{:S(2)}) async-start(), calls=%async_computation.3 | async-start | bytes 2359296 | tf_op jit(solution)/shard_map/reduce_scatter | solution.py:135
  38.3 2.5 %copy-start.2 = (bf16[1,1,32,2,64,64]{5,4,3,2,1,0:T(8,128)(2,1)S(1)}, bf16[1,1,32,2,64,64]{5,4,3,2,1,0:T(8,128)(2,1)}, u32[]{:S(2)}) copy-start(bf16[1,1,32,2,64,64]{5,4,3,2,1,0:T(8,128)(2,1)} %get-tuple-element.20) | copy-start | bytes 1572868
  40.8 1.2 copy-start.12
  41.4 1.8 %copy-start.14 = (bf16[1,1,32,2,64,64]{5,4,3,2,1,0:T(8,128)(2,1)S(1)}, bf16[1,1,32,2,64,64]{5,4,3,2,1,0:T(8,128)(2,1)}, u32[]{:S(2)}) copy-start(bf16[1,1,32,2,64,64]{5,4,3,2,1,0:T(8,128)(2,1)} %get-tuple-element.12) | copy-start | bytes 1572868
  43.1 1.2 copy-start.16
  64.3 2.1 %copy-start.17 = (bf16[1,1,32,2,64,64]{5,4,3,2,1,0:T(8,128)(2,1)S(1)}, bf16[1,1,32,2,64,64]{5,4,3,2,1,0:T(8,128)(2,1)}, u32[]{:S(2)}) copy-start(bf16[1,1,32,2,64,64]{5,4,3,2,1,0:T(8,128)(2,1)} %get-tuple-element.13) | copy-start | bytes 1572868
  66.4 1.2 copy-start.15
  67.6 1.2 copy-start.13
  68.8 1.2 copy-start.3
  70.1 1.5 %copy-start.4 = (bf16[1,32,128,64]{2,3,1,0:T(8,128)(2,1)S(1)}, bf16[1,32,128,64]{2,3,1,0:T(8,128)(2,1)}, u32[]{:S(2)}) copy-start(bf16[1,32,128,64]{2,3,1,0:T(8,128)(2,1)} %param.9) | copy-start | bytes 1572868
  77.0 32.7 %all-to-all-start.1 = ((bf16[1,32,64,256]{3,2,0,1:T(8,128)(2,1)}), bf16[1,32,64,256]{3,2,0,1:T(8,128)(2,1)}, u32[]{:S(2)}, u32[]{:S(2)}) async-start(bf16[1,32,64,256]{3,2,0,1:T(8,128)(2,1)} %bitcast.364), calls=%async_computation.2 | async-start | bytes 2097152 | tf_op jit(solution)/shard_map/all_to_all | solution.py:126
  109.7 2.4 %copy-start.11 = (bf16[1,1,32,2,64,64]{5,4,3,2,1,0:T(8,128)(2,1)S(1)}, bf16[1,1,32,2,64,64]{5,4,3,2,1,0:T(8,128)(2,1)}, u32[]{:S(2)}) copy-start(bf16[1,1,32,2,64,64]{5,4,3,2,1,0:T(8,128)(2,1)} %get-tuple-element.16) | copy-start | bytes 1572868
  112.1 1.2 copy-start.9
  113.2 1.3 copy-start.7
  115.6 1.7 %copy-start.5 = (bf16[1,32,128,64]{2,3,1,0:T(8,128)(2,1)S(1)}, bf16[1,32,128,64]{2,3,1,0:T(8,128)(2,1)}, u32[]{:S(2)}) copy-start(bf16[1,32,128,64]{2,3,1,0:T(8,128)(2,1)} %param.8) | copy-start | bytes 1572868
Sparse Core Ops, SparseCore 0:
  73.8 30.1 reduce-scatter.1
where the time goes:
time: 127 us; the launch traced here: 126 us
  waiting for transfers between devices  43.8 us (34%)
  matrix products  32.5 us (26%)
  starting transfers between devices  17.4 us (14%)
  between operations  14.5 us (11%)
  local copies, waits for them, and re-layouts  13.9 us (11%)
  other arithmetic  4.07 us (3%)
    all_to_all x1, waiting for transfers between devices, body(): lax.all_to_all(upper, 'lvl', split_axis=1, concat_axis=0, tiled=True)  25.8 us
    all_to_all x1, waiting for transfers between devices, body(): lax.all_to_all(lower, 'lvl', split_axis=1, concat_axis=0, tiled=True)  18 us
    all_to_all x1, starting transfers between devices, body(): lax.all_to_all(lower, 'lvl', split_axis=1, concat_axis=0, tiled=True)  11.7 us
    dot_general x5, matrix products, adjoint_high(): jnp.einsum('hbjcrs,hbjrk->hjcsk', level_tiles, current, preferred_element...  7.9 us
    slice x1, local copies, waits for them, and re-layouts, forward_high(): tiles_all[height - 1]  7.87 us
    dot_general x5, matrix products, adjoint_low(): jnp.einsum('jhbcrs,hbjrk->hjcsk', level_tiles, current, preferred_element...  6.75 us
    dot_general x5, matrix products, forward_high(): jnp.einsum('hbjcrs,jchsk->jhbrk', level_tiles, before, preferred_element_...  5.72 us
    all_to_all x1, starting transfers between devices, body(): lax.all_to_all(upper, 'lvl', split_axis=1, concat_axis=0, tiled=True)  5.63 us
  transfers between devices with their start and end apart: 3, of which 2 were waited for; matrix products, arithmetic and copies ran while one was open for 18% of the time, Pallas kernels for 0%

commit v1 on v0

v1 whole, which is shorter than its diff:
```python
import jax
import jax.numpy as jnp
from jax import lax
from jax.experimental import pallas as pl
from jax.experimental.pallas import tpu as pltpu
from jax.sharding import PartitionSpec as P

LEVELS = 10
MIDDLE = LEVELS // 2
LEAF = 128
RANK = 64
HALF = RANK // 2
NRHS = 256
NODES = 32
PAIRS = NODES // 2
GROUPS = 8
CHIPS = GROUPS // 2
SHARE = NODES // GROUPS
UNROLL = 4
MESH = pl.DeviceIdType.MESH
F32 = jnp.float32
BF16 = jnp.bfloat16


def kernel(
    right_hbm, rows_hbm, basis_in_hbm, basis_out_hbm, tiles_hbm, ranks,
    row_out, col_out,
    right, rows, basis_in, basis_out, tiles, ping, pong,
    send_f, recv_f, send_a, recv_a,
    part, swap, pair_sum, gathered, row_buf, col_buf,
    load_sem, tile_sem, store_sem, row_sem,
    ssem_f, rsem_f, ssem_a, rsem_a, ssem_c, rsem_c, ssem_y, rsem_y,
):
    me = lax.axis_index("lvl")
    blk = lax.axis_index("blk")
    core = lax.rem(blk, 2)
    chip = blk // 2
    my_pair = me // 2

    quarter = NODES // 4
    loads = {}
    for name, src, dst, base in (
        ("right", right_hbm, right, 0),
        ("rows", rows_hbm, rows, 4),
        ("basis_in", basis_in_hbm, basis_in, 8),
        ("basis_out", basis_out_hbm, basis_out, 9),
    ):
        if base < 8:
            loads[name] = [
                pltpu.make_async_copy(
                    src.at[pl.ds(c * quarter, quarter)],
                    dst.at[pl.ds(c * quarter, quarter)],
                    load_sem.at[base + c],
                )
                for c in range(4)
            ]
        else:
            loads[name] = [pltpu.make_async_copy(src, dst, load_sem.at[base])]
    tile_loads = [
        pltpu.make_async_copy(tiles_hbm.at[l], tiles.at[l], tile_sem.at[l]) for l in range(LEVELS)
    ]
    for copy in loads["basis_in"] + loads["right"] + tile_loads[:MIDDLE]:
        copy.start()
    for copy in loads["basis_out"] + loads["rows"] + tile_loads[: MIDDLE - 1 : -1]:
        copy.start()

    barrier = pltpu.get_barrier_semaphore()

    def greet(k, carry):
        pl.semaphore_signal(
            barrier, inc=1, device_id=(lax.rem(me + k, NODES), blk), device_id_type=MESH
        )
        return carry

    lax.fori_loop(1, NODES, greet, 0)
    for k in range(1, CHIPS):
        other = lax.rem(chip + k, CHIPS) * 2 + core
        pl.semaphore_signal(barrier, inc=1, device_id=(me, other), device_id_type=MESH)
    pl.semaphore_signal(
        barrier, inc=1, device_id=(me, chip * 2 + 1 - core), device_id_type=MESH
    )

    def loop(count, body, unroll=UNROLL):
        def step(t, carry):
            for u in range(unroll):
                body(t * unroll + u)
            return carry

        lax.fori_loop(0, count // unroll, step, 0)

    def keep(level, node, values):
        return jnp.where(ranks[level, 0, node] > HALF, values, jnp.zeros_like(values))

    def put_node(ref, node, values, level=None, rank_node=None):
        ref[node, 0:HALF] = values[0:HALF].astype(BF16)
        low = values[HALF:RANK]
        if level is not None:
            low = keep(level, rank_node, low)
        ref[node, HALF:RANK] = low.astype(BF16)

    def matrix(level, first, second):
        t = tiles
        return jnp.concatenate(
            [
                jnp.concatenate([t[level - 1, node, 0], t[level - 1, node, 1]], axis=1)
                for node in (first, second)
            ],
            axis=0,
        )

    def two(ref, first, second):
        return jnp.concatenate([ref[first], ref[second]], axis=0)

    def apply(w, x):
        return jnp.dot(w, x, preferred_element_type=F32)

    def apply_t(w, x):
        return lax.dot_general(w, x, (((0,), (0,)), ((), ())), preferred_element_type=F32)

    def copy_f(q, node):
        return pltpu.make_async_remote_copy(
            send_f.at[q], recv_f.at[node], ssem_f.at[q], rsem_f.at[node],
            device_id=(q, blk), device_id_type=MESH,
        )

    def copy_a(q, node):
        return pltpu.make_async_remote_copy(
            send_a.at[q], recv_a.at[node], ssem_a.at[q], rsem_a.at[node],
            device_id=(q, blk), device_id_type=MESH,
        )

    def hand_over(q, send, recv, copy):
        @pl.when(q != me)
        def _():
            copy(q, me).start()

        @pl.when(q == me)
        def _():
            recv[me] = send[q]

    def arrived(q, copy):
        @pl.when(q != me)
        def _():
            copy(q, q).wait_recv()

    loads["basis_in"][0].wait()
    for c in range(4):
        loads["right"][c].wait()

        def leaf(n, c=c):
            n = c * quarter + n
            put_node(ping, n, apply(basis_in[n], right[n]), 0, n)

        loop(quarter, leaf)
    src, dst = ping, pong
    for level in range(1, MIDDLE):
        tile_loads[level - 1].wait()
        span = 2 ** (level - 1)

        def low(t, level=level, span=span, src=src, dst=dst):
            j, h = t // span, lax.rem(t, span)
            at = 2 * j * span + h
            out = apply(matrix(level, 2 * t, 2 * t + 1), two(src, at, at + span))
            put_node(dst, 2 * t, out[:RANK], level, 2 * t)
            put_node(dst, 2 * t + 1, out[RANK:], level, 2 * t + 1)

        loop(PAIRS, low)
        src, dst = dst, src
    tile_loads[MIDDLE - 1].wait()
    pl.semaphore_wait(barrier, NODES - 1 + CHIPS)

    def low_last(k, src=src):
        h = jnp.bitwise_xor(my_pair, k)
        out = apply(matrix(MIDDLE, 2 * h, 2 * h + 1), two(src, h, h + PAIRS))
        put_node(send_f, 2 * h, out[:RANK], MIDDLE, 2 * h)
        put_node(send_f, 2 * h + 1, out[RANK:], MIDDLE, 2 * h + 1)
        hand_over(2 * h, send_f, recv_f, copy_f)
        hand_over(2 * h + 1, send_f, recv_f, copy_f)

    loop(PAIRS, low_last, 2)

    loads["basis_out"][0].wait()
    for c in range(4):
        loads["rows"][c].wait()

        def row_leaf(n, c=c):
            n = c * quarter + n
            put_node(ping, n, apply(basis_out[n], rows[n]), LEVELS, n)

        loop(quarter, row_leaf)
    src, dst = ping, pong
    for level in range(LEVELS, MIDDLE + 1, -1):
        tile_loads[level - 1].wait()
        width = 2 ** (LEVELS - level)

        def high_t(u, level=level, width=width, src=src, dst=dst):
            h, j = u // width, lax.rem(u, width)
            first = 2 * h * width + j
            out = apply_t(matrix(level, first, first + width), two(src, first, first + width))
            put_node(dst, 2 * u, out[:RANK], level - 1, 2 * u)
            put_node(dst, 2 * u + 1, out[RANK:], level - 1, 2 * u + 1)

        loop(PAIRS, high_t)
        src, dst = dst, src
    tile_loads[MIDDLE].wait()

    def high_t_last(k, src=src):
        j = jnp.bitwise_xor(my_pair, k)
        out = apply_t(matrix(MIDDLE + 1, j, j + PAIRS), two(src, j, j + PAIRS))
        put_node(send_a, 2 * j, out[:RANK])
        put_node(send_a, 2 * j + 1, out[RANK:])
        hand_over(2 * j, send_a, recv_a, copy_a)
        hand_over(2 * j + 1, send_a, recv_a, copy_a)

    loop(PAIRS, high_t_last, 2)

    def high_first(k, dst=ping):
        j = jnp.bitwise_xor(my_pair, k)
        arrived(2 * j, copy_f)
        arrived(2 * j + 1, copy_f)
        out = apply(matrix(MIDDLE + 1, j, j + PAIRS), two(recv_f, 2 * j, 2 * j + 1))
        put_node(dst, j, out[:RANK], MIDDLE + 1, j)
        put_node(dst, j + PAIRS, out[RANK:], MIDDLE + 1, j + PAIRS)

    loop(PAIRS, high_first, 2)
    src, dst = ping, pong
    for level in range(MIDDLE + 2, LEVELS + 1):
        width = 2 ** (LEVELS - level)

        def high(u, level=level, width=width, src=src, dst=dst):
            h, j = u // width, lax.rem(u, width)
            first = 2 * h * width + j
            out = apply(matrix(level, first, first + width), two(src, 2 * u, 2 * u + 1))
            put_node(dst, first, out[:RANK], level, first)
            put_node(dst, first + width, out[RANK:], level, first + width)

        loop(PAIRS, high)
        src, dst = dst, src

    def swap_copy(y):
        group = 2 * y + 1 - core
        return pltpu.make_async_remote_copy(
            part.at[pl.ds(SHARE * group, SHARE)], swap.at[y], ssem_c.at[y], rsem_c.at[y],
            device_id=(me, chip * 2 + 1 - core), device_id_type=MESH,
        )

    def y_copy(y, slot):
        return pltpu.make_async_remote_copy(
            pair_sum.at[y], gathered.at[slot], ssem_y.at[y], rsem_y.at[slot],
            device_id=(me, 2 * y + core), device_id_type=MESH,
        )

    def row_leaf_out(group, src=src):
        for s in range(SHARE):
            n = SHARE * group + s
            part[n] = apply_t(basis_out[n], src[n]).astype(BF16)

    def for_sibling(y, carry):
        row_leaf_out(2 * y + 1 - core)
        swap_copy(y).start()
        return carry

    lax.fori_loop(0, CHIPS, for_sibling, 0)

    def for_core(y, carry):
        row_leaf_out(2 * y + core)
        return carry

    lax.fori_loop(0, CHIPS, for_core, 0)

    def exchange(k, carry):
        y = lax.rem(chip + k, CHIPS)
        swap_copy(y).wait_recv()
        group = 2 * y + core
        for s in range(SHARE):
            pair_sum[y, s] = (
                part[SHARE * group + s].astype(F32) + swap[y, s].astype(F32)
            ).astype(BF16)

        @pl.when(y != chip)
        def _():
            y_copy(y, chip).start()

        return carry

    lax.fori_loop(1, CHIPS + 1, exchange, 0)

    def low_t_first(k, dst=ping):
        h = jnp.bitwise_xor(my_pair, k)
        arrived(2 * h, copy_a)
        arrived(2 * h + 1, copy_a)
        pieces = []
        for node in (2 * h, 2 * h + 1):
            pieces.append(recv_a[node, 0:HALF])
            pieces.append(keep(MIDDLE, node, recv_a[node, HALF:RANK]))
        out = apply_t(matrix(MIDDLE, 2 * h, 2 * h + 1), jnp.concatenate(pieces, axis=0))
        put_node(dst, h, out[:RANK], MIDDLE - 1, h)
        put_node(dst, h + PAIRS, out[RANK:], MIDDLE - 1, h + PAIRS)

    loop(PAIRS, low_t_first, 2)

    for k in range(1, CHIPS):
        y = lax.rem(chip + k, CHIPS)
        y_copy(y, y).wait_recv()
    for s in range(SHARE):
        total = pair_sum[chip, s].astype(F32)
        for k in range(1, CHIPS):
            total = total + gathered[lax.rem(chip + k, CHIPS), s].astype(F32)
        row_buf[s] = total.astype(BF16)
    row_store = pltpu.make_async_copy(row_buf, row_out, row_sem)
    row_store.start()

    src, dst = ping, pong
    for level in range(MIDDLE - 1, 0, -1):
        span = 2 ** (level - 1)

        def low_t(t, level=level, span=span, src=src, dst=dst):
            j, h = t // span, lax.rem(t, span)
            at = 2 * j * span + h
            out = apply_t(matrix(level, 2 * t, 2 * t + 1), two(src, 2 * t, 2 * t + 1))
            put_node(dst, at, out[:RANK], level - 1, at)
            put_node(dst, at + span, out[RANK:], level - 1, at + span)

        loop(PAIRS, low_t)
        src, dst = dst, src
    stores = []
    for c in range(4):

        def leaf_out(n, c=c, src=src):
            n = c * quarter + n
            col_buf[n] = apply_t(basis_in[n], src[n]).astype(BF16)

        loop(quarter, leaf_out)
        stores.append(
            pltpu.make_async_copy(
                col_buf.at[pl.ds(c * quarter, quarter)],
                col_out.at[pl.ds(c * quarter, quarter)],
                store_sem.at[c],
            )
        )
        stores[-1].start()

    def sent(k, carry):
        q = lax.rem(me + k, NODES)
        copy_f(q, me).wait_send()
        copy_a(q, me).wait_send()
        return carry

    lax.fori_loop(1, NODES, sent, 0)
    for y in range(CHIPS):
        swap_copy(y).wait_send()
    for k in range(1, CHIPS):
        y_copy(lax.rem(chip + k, CHIPS), chip).wait_send()
    for copy in stores:
        copy.wait()
    row_store.wait()


def body(right_sides, row_vectors, leaf_basis_in, leaf_basis_out, transfers, tile_ranks):
    hbm = pl.BlockSpec(memory_space=pl.ANY)
    nodes = (NODES, RANK, NRHS)
    leaves = (NODES, LEAF, NRHS)
    dma = pltpu.SemaphoreType.DMA
    row, col = pl.pallas_call(
        kernel,
        out_shape=(
            jax.ShapeDtypeStruct((SHARE, LEAF, NRHS), BF16),
            jax.ShapeDtypeStruct(leaves, BF16),
        ),
        in_specs=[hbm] * 5 + [pl.BlockSpec(memory_space=pltpu.SMEM)],
        out_specs=(hbm, hbm),
        scratch_shapes=[
            pltpu.VMEM(leaves, BF16),
            pltpu.VMEM(leaves, BF16),
            pltpu.VMEM((NODES, RANK, LEAF), BF16),
            pltpu.VMEM((NODES, RANK, LEAF), BF16),
            pltpu.VMEM((LEVELS, NODES, 2, RANK, RANK), BF16),
            pltpu.VMEM(nodes, BF16),
            pltpu.VMEM(nodes, BF16),
            pltpu.VMEM(nodes, BF16),
            pltpu.VMEM(nodes, BF16),
            pltpu.VMEM(nodes, BF16),
            pltpu.VMEM(nodes, BF16),
            pltpu.VMEM(leaves, BF16),
            pltpu.VMEM((CHIPS, SHARE, LEAF, NRHS), BF16),
            pltpu.VMEM((CHIPS, SHARE, LEAF, NRHS), BF16),
            pltpu.VMEM((CHIPS, SHARE, LEAF, NRHS), BF16),
            pltpu.VMEM((SHARE, LEAF, NRHS), BF16),
            pltpu.VMEM(leaves, BF16),
            dma((10,)),
            dma((LEVELS,)),
            dma((4,)),
            dma,
            dma((NODES,)),
            dma((NODES,)),
            dma((NODES,)),
            dma((NODES,)),
            dma((CHIPS,)),
            dma((CHIPS,)),
            dma((CHIPS,)),
            dma((CHIPS,)),
        ],
        compiler_params=pltpu.CompilerParams(
            collective_id=0, has_side_effects=True, vmem_limit_bytes=56 << 20
        ),
        name="butterfly",
    )(
        right_sides.reshape(leaves),
        row_vectors.reshape(leaves),
        jnp.swapaxes(leaf_basis_in[0], 1, 2),
        jnp.swapaxes(leaf_basis_out[0], 1, 2),
        transfers[0],
        jnp.swapaxes(tile_ranks, 0, 1),
    )
    return row.reshape(SHARE * LEAF, NRHS), col.reshape(1, NODES * LEAF, NRHS)


def solution(mesh):
    return jax.shard_map(
        body,
        mesh=mesh,
        in_specs=(
            P("blk", "lvl", None),
            P("lvl", None),
            P("blk", "lvl", None, None),
            P("blk", "lvl", None, None),
            P("blk", None, "lvl", None, None, None),
            P("blk", None, "lvl"),
        ),
        out_specs=(P(("lvl", "blk"), None), P("blk", "lvl", None)),
        check_vma=False,
    )
```

time: 127 us -> 83.5 us (0.66)
  the two profiles are of different devices: /device:TPU:10 before, /device:TPU:1 now
where the time goes in v1:
time: 83.5 us; the launch traced here: 83.4 us
  Pallas kernels  78 us (93%)
  local copies, waits for them, and re-layouts  4.71 us (6%)
    pallas_call x1, Pallas kernels, body(): pl.pallas_call(kernel, out_shape=(jax.ShapeDtypeStruct((SHARE, LEAF, NRHS...  78 us
    unnamed x2, local copies, waits for them, and re-layouts  4.71 us

profile of v1, /device:TPU:1, one launch (start us, length us, event | category | flops | bytes accessed | tf_op | source)
XLA Modules:
  0.0 83.4 jit_solution(4175956333506199511)
XLA Ops:
  0.6 78.0 %butterfly.1 = (bf16[4,128,256]{2,1,0:T(8,128)(2,1)}, bf16[32,128,256]{2,1,0:T(8,128)(2,1)}) custom-call(bf16[32,128,256]{2,1,0:T(8,128)(2,1)} %bitcast.13, bf16[32,128,256]{2,1,0:T(8,128)(2,1)} %bitcast.14, bf16[32,64,128]{2,1,0:T(8,128)(2,1)} %bitcast.16, bf16[32,64,128]{2,1,0:T(8,128)(2,1)} %bitcast.17, bf16[10,32,2,64,64]{4,3,2,1,0:T(8,128)(2,1)} %bitcast.12, ...), custom_call_target="tpu_custom_call" | custom-call | tf_op jit(solution)/shard_map/butterfly/pallas_call | solution.py:364
  78.6 1.7 %copy.10 = bf16[512,256]{1,0:T(8,128)(2,1)} copy(bf16[512,256]{1,0:T(8,128)(2,1)} %bitcast.18) | data formatting | bytes 524288
  80.3 3.0 %copy.11 = bf16[1,4096,256]{2,1,0:T(8,128)(2,1)} copy(bf16[1,4096,256]{2,1,0:T(8,128)(2,1)} %bitcast.15) | data formatting | bytes 4194304

commit v2 on v1

v2 whole, which is shorter than its diff:
```python
import jax
import jax.numpy as jnp
from jax import lax
from jax.experimental import pallas as pl
from jax.experimental.pallas import tpu as pltpu
from jax.sharding import PartitionSpec as P

LEVELS = 10
MIDDLE = LEVELS // 2
LEAF = 128
RANK = 64
HALF = RANK // 2
NRHS = 256
NODES = 32
PAIRS = NODES // 2
GROUPS = 8
CHIPS = GROUPS // 2
SHARE = NODES // GROUPS
MESH = pl.DeviceIdType.MESH
F32 = jnp.float32
BF16 = jnp.bfloat16


def kernel(
    right_hbm, rows_hbm, basis_in, basis_out, tiles_hbm, ranks,
    row_out, col_out,
    right, rows, tiles, turned, ping, pong,
    send_f, recv_f, send_a, recv_a,
    part, swap, pair_sum, gathered,
    load_sem, tile_sem,
    ssem_f, rsem_f, ssem_a, rsem_a, ssem_c, rsem_c, ssem_y, rsem_y,
):
    me = lax.axis_index("lvl")
    blk = lax.axis_index("blk")
    core = lax.rem(blk, 2)
    chip = blk // 2
    my_pair = me // 2

    quarter = NODES // 4
    loads = {}
    for name, src, dst, base in (("right", right_hbm, right, 0), ("rows", rows_hbm, rows, 4)):
        loads[name] = [
            pltpu.make_async_copy(
                src.at[pl.ds(c * quarter, quarter)],
                dst.at[pl.ds(c * quarter, quarter)],
                load_sem.at[base + c],
            )
            for c in range(4)
        ]
    tile_loads = [
        pltpu.make_async_copy(tiles_hbm.at[l], tiles.at[l], tile_sem.at[l]) for l in range(LEVELS)
    ]
    for copy in loads["right"] + tile_loads[:MIDDLE]:
        copy.start()
    for copy in loads["rows"] + tile_loads[: MIDDLE - 1 : -1]:
        copy.start()

    barrier = pltpu.get_barrier_semaphore()

    def greet(k, carry):
        pl.semaphore_signal(
            barrier, inc=1, device_id=(lax.rem(me + k, NODES), blk), device_id_type=MESH
        )
        return carry

    lax.fori_loop(1, NODES, greet, 0)
    for k in range(1, CHIPS):
        other = lax.rem(chip + k, CHIPS) * 2 + core
        pl.semaphore_signal(barrier, inc=1, device_id=(me, other), device_id_type=MESH)
    pl.semaphore_signal(
        barrier, inc=1, device_id=(me, chip * 2 + 1 - core), device_id_type=MESH
    )

    def keep(level, node, values):
        return jnp.where(ranks[level, 0, node] > HALF, values, jnp.zeros_like(values))

    def put_node(ref, node, values, level=None):
        ref[node, 0:HALF] = values[0:HALF].astype(BF16)
        low = values[HALF:RANK]
        if level is not None:
            low = keep(level, node, low)
        ref[node, HALF:RANK] = low.astype(BF16)

    def put_pair(ref, first, second, out, level=None):
        put_node(ref, first, out[:RANK], level)
        put_node(ref, second, out[RANK:], level)

    def matrix(level, first, second):
        return jnp.concatenate(
            [
                jnp.concatenate([tiles[level - 1, node, 0], tiles[level - 1, node, 1]], axis=1)
                for node in (first, second)
            ],
            axis=0,
        )

    def two(ref, first, second):
        return jnp.concatenate([ref[first], ref[second]], axis=0)

    def apply(w, x):
        return jnp.dot(w, x, preferred_element_type=F32)

    def apply_t(w, x):
        return lax.dot_general(w, x, (((0,), (0,)), ((), ())), preferred_element_type=F32)

    def copy_f(q, node):
        return pltpu.make_async_remote_copy(
            send_f.at[q], recv_f.at[node], ssem_f.at[q], rsem_f.at[node],
            device_id=(q, blk), device_id_type=MESH,
        )

    def copy_a(q, node):
        return pltpu.make_async_remote_copy(
            send_a.at[q], recv_a.at[node], ssem_a.at[q], rsem_a.at[node],
            device_id=(q, blk), device_id_type=MESH,
        )

    def peer(k):
        return jnp.bitwise_xor(me, k)

    def send(copy, first, last):
        def step(k, carry):
            copy(peer(k), me).start()
            return carry

        lax.fori_loop(max(first, 1), last, step, 0)

    def await_from(copy, first, last):
        def step(k, carry):
            copy(me, peer(k)).wait_recv()
            return carry

        lax.fori_loop(max(first, 1), last, step, 0)

    for c in range(4):
        loads["right"][c].wait()
        for n in range(c * quarter, (c + 1) * quarter):
            put_node(ping, n, apply(basis_in[n], right[n]), 0)
    src, dst = ping, pong
    for level in range(1, MIDDLE):
        tile_loads[level - 1].wait()
        span = 2 ** (level - 1)
        for t in range(PAIRS):
            at = 2 * (t // span) * span + t % span
            out = apply(matrix(level, 2 * t, 2 * t + 1), two(src, at, at + span))
            put_pair(dst, 2 * t, 2 * t + 1, out, level)
        src, dst = dst, src
    tile_loads[MIDDLE - 1].wait()
    pl.semaphore_wait(barrier, NODES - 1 + CHIPS)
    for part_k in (1, 0):
        for k in range(part_k * 8, part_k * 8 + 8):
            h = jnp.bitwise_xor(my_pair, k)
            out = apply(matrix(MIDDLE, 2 * h, 2 * h + 1), two(src, h, h + PAIRS))
            put_pair(send_f, 2 * h, 2 * h + 1, out, MIDDLE)
        send(copy_f, 16 * part_k, 16 * part_k + 16)
    recv_f[me] = send_f[me]

    for c in range(4):
        loads["rows"][c].wait()
        for n in range(c * quarter, (c + 1) * quarter):
            put_node(ping, n, apply(basis_out[n], rows[n]), LEVELS)
    src, dst = ping, pong
    for level in range(LEVELS, MIDDLE + 1, -1):
        tile_loads[level - 1].wait()
        width = 2 ** (LEVELS - level)
        for u in range(PAIRS):
            first = 2 * (u // width) * width + u % width
            out = apply_t(matrix(level, first, first + width), two(src, first, first + width))
            put_pair(dst, 2 * u, 2 * u + 1, out, level - 1)
        src, dst = dst, src
    tile_loads[MIDDLE].wait()
    for part_k in (1, 0):
        for k in range(part_k * 8, part_k * 8 + 8):
            j = jnp.bitwise_xor(my_pair, k)
            out = apply_t(matrix(MIDDLE + 1, j, j + PAIRS), two(src, j, j + PAIRS))
            put_pair(send_a, 2 * j, 2 * j + 1, out)
        send(copy_a, 16 * part_k, 16 * part_k + 16)
    recv_a[me] = send_a[me]

    for level in range(1, MIDDLE + 1):
        span = 2 ** (level - 1)
        for t in range(PAIRS):
            at = 2 * (t // span) * span + t % span
            w = matrix(level, 2 * t, 2 * t + 1)
            if level == MIDDLE:
                w = jnp.concatenate(
                    [
                        w[0:HALF], keep(level, 2 * t, w[HALF:RANK]),
                        w[RANK : RANK + HALF], keep(level, 2 * t + 1, w[RANK + HALF :]),
                    ],
                    axis=0,
                )
            w = w.T
            turned[level - 1, t, 0:HALF] = w[0:HALF]
            turned[level - 1, t, HALF:RANK] = keep(level - 1, at, w[HALF:RANK])
            turned[level - 1, t, RANK : RANK + HALF] = w[RANK : RANK + HALF]
            turned[level - 1, t, RANK + HALF :] = keep(level - 1, at + span, w[RANK + HALF :])

    await_from(copy_f, 0, NODES)
    src, dst = recv_f, ping
    for level in range(MIDDLE + 1, LEVELS + 1):
        width = 2 ** (LEVELS - level)
        for u in range(PAIRS):
            first = 2 * (u // width) * width + u % width
            out = apply(matrix(level, first, first + width), two(src, 2 * u, 2 * u + 1))
            put_pair(dst, first, first + width, out, level)
        src, dst = dst, (pong if dst is ping else ping)

    def swap_copy(y):
        group = 2 * y + 1 - core
        return pltpu.make_async_remote_copy(
            part.at[pl.ds(SHARE * group, SHARE)], swap.at[y], ssem_c.at[y], rsem_c.at[y],
            device_id=(me, chip * 2 + 1 - core), device_id_type=MESH,
        )

    def y_copy(y, slot):
        return pltpu.make_async_remote_copy(
            pair_sum.at[y], gathered.at[slot], ssem_y.at[y], rsem_y.at[slot],
            device_id=(me, 2 * y + core), device_id_type=MESH,
        )

    def row_leaf_out(group):
        for s in range(SHARE):
            n = SHARE * group + s
            part[n] = apply_t(basis_out[n], src[n]).astype(BF16)

    for y in range(CHIPS):
        row_leaf_out(2 * y + 1 - core)
        swap_copy(y).start()
    for y in range(CHIPS):
        row_leaf_out(2 * y + core)

    def add_pair(y):
        swap_copy(y).wait_recv()
        group = 2 * y + core
        for s in range(SHARE):
            pair_sum[y, s] = (
                part[SHARE * group + s].astype(F32) + swap[y, s].astype(F32)
            ).astype(BF16)

    def exchange(k, carry):
        y = lax.rem(chip + k, CHIPS)
        add_pair(y)
        y_copy(y, chip).start()
        return carry

    lax.fori_loop(1, CHIPS, exchange, 0)
    add_pair(chip)

    for part_k in range(4):
        if part_k == 3:
            for k in range(1, CHIPS):
                y = lax.rem(chip + k, CHIPS)
                y_copy(y, y).wait_recv()
            for s in range(SHARE):
                total = pair_sum[chip, s].astype(F32)
                for k in range(1, CHIPS):
                    total = total + gathered[lax.rem(chip + k, CHIPS), s].astype(F32)
                row_out[s] = total.astype(BF16)
        group_k = 3 - part_k
        await_from(copy_a, 8 * group_k, 8 * group_k + 8)
        for k in range(4 * group_k, 4 * group_k + 4):
            h = jnp.bitwise_xor(my_pair, k)
            out = apply(turned[MIDDLE - 1, h], two(recv_a, 2 * h, 2 * h + 1)).astype(BF16)
            ping[h] = out[:RANK]
            ping[h + PAIRS] = out[RANK:]
    src, dst = ping, pong
    for level in range(MIDDLE - 1, 0, -1):
        span = 2 ** (level - 1)
        for t in range(PAIRS):
            at = 2 * (t // span) * span + t % span
            out = apply(turned[level - 1, t], two(src, 2 * t, 2 * t + 1)).astype(BF16)
            dst[at] = out[:RANK]
            dst[at + span] = out[RANK:]
        src, dst = dst, src
    for n in range(NODES):
        col_out[n] = apply_t(basis_in[n], src[n]).astype(BF16)

    def sent(k, carry):
        copy_f(peer(k), me).wait_send()
        copy_a(peer(k), me).wait_send()
        return carry

    lax.fori_loop(1, NODES, sent, 0)
    for y in range(CHIPS):
        swap_copy(y).wait_send()
    for k in range(1, CHIPS):
        y_copy(lax.rem(chip + k, CHIPS), chip).wait_send()


def body(right_sides, row_vectors, leaf_basis_in, leaf_basis_out, transfers, tile_ranks):
    hbm = pl.BlockSpec(memory_space=pl.ANY)
    vmem = pl.BlockSpec(memory_space=pltpu.VMEM)
    nodes = (NODES, RANK, NRHS)
    leaves = (NODES, LEAF, NRHS)
    dma = pltpu.SemaphoreType.DMA
    row, col = pl.pallas_call(
        kernel,
        out_shape=(
            jax.ShapeDtypeStruct((SHARE, LEAF, NRHS), BF16),
            jax.ShapeDtypeStruct(leaves, BF16),
        ),
        in_specs=[hbm, hbm, vmem, vmem, hbm, pl.BlockSpec(memory_space=pltpu.SMEM)],
        out_specs=(vmem, vmem),
        scratch_shapes=[
            pltpu.VMEM(leaves, BF16),
            pltpu.VMEM(leaves, BF16),
            pltpu.VMEM((LEVELS, NODES, 2, RANK, RANK), BF16),
            pltpu.VMEM((MIDDLE, PAIRS, 2 * RANK, 2 * RANK), BF16),
            pltpu.VMEM(nodes, BF16),
            pltpu.VMEM(nodes, BF16),
            pltpu.VMEM(nodes, BF16),
            pltpu.VMEM(nodes, BF16),
            pltpu.VMEM(nodes, BF16),
            pltpu.VMEM(nodes, BF16),
            pltpu.VMEM(leaves, BF16),
            pltpu.VMEM((CHIPS, SHARE, LEAF, NRHS), BF16),
            pltpu.VMEM((CHIPS, SHARE, LEAF, NRHS), BF16),
            pltpu.VMEM((CHIPS, SHARE, LEAF, NRHS), BF16),
            dma((8,)),
            dma((LEVELS,)),
            dma((NODES,)),
            dma((NODES,)),
            dma((NODES,)),
            dma((NODES,)),
            dma((CHIPS,)),
            dma((CHIPS,)),
            dma((CHIPS,)),
            dma((CHIPS,)),
        ],
        compiler_params=pltpu.CompilerParams(
            collective_id=0, has_side_effects=True, vmem_limit_bytes=50 << 20
        ),
        name="butterfly",
    )(
        right_sides.reshape(leaves),
        row_vectors.reshape(leaves),
        jnp.swapaxes(leaf_basis_in[0], 1, 2),
        jnp.swapaxes(leaf_basis_out[0], 1, 2),
        transfers[0],
        jnp.swapaxes(tile_ranks, 0, 1),
    )
    return row.reshape(SHARE * LEAF, NRHS), col.reshape(1, NODES * LEAF, NRHS)


def solution(mesh):
    return jax.shard_map(
        body,
        mesh=mesh,
        in_specs=(
            P("blk", "lvl", None),
            P("lvl", None),
            P("blk", "lvl", None, None),
            P("blk", "lvl", None, None),
            P("blk", None, "lvl", None, None, None),
            P("blk", None, "lvl"),
        ),
        out_specs=(P(("lvl", "blk"), None), P("blk", "lvl", None)),
        check_vma=False,
    )
```

time: 83.5 us -> 77.5 us (0.928); the launches traced: 83.4 us -> 76.4 us
  Pallas kernels: 78 us -> 71 us
    pallas_call x1, Pallas kernels: 78 us -> 71 us  [body(): pl.pallas_call(kernel, out_shape=(jax.ShapeDtypeStruct((SHARE, LEAF, NRHS...]
    unnamed x2 -> x8, local copies, waits for them, and re-layouts: 4.71 us -> 4.79 us
where the time goes in v2:
time: 77.5 us; the launch traced here: 76.4 us
  Pallas kernels  71 us (92%)
  local copies, waits for them, and re-layouts  4.79 us (6%)
    pallas_call x1, Pallas kernels, body(): pl.pallas_call(kernel, out_shape=(jax.ShapeDtypeStruct((SHARE, LEAF, NRHS...  71 us
    unnamed x8, local copies, waits for them, and re-layouts  4.79 us

profile of v2, /device:TPU:1, one launch (start us, length us, event | category | flops | bytes accessed | tf_op | source)
XLA Modules:
  0.0 76.4 jit_solution(9616566925130255325)
XLA Ops:
  0.6 0.0 copy-start
  0.6 1.0 %copy-done = bf16[1,32,128,64]{2,3,1,0:T(8,128)(2,1)S(1)} copy-done((bf16[1,32,128,64]{2,3,1,0:T(8,128)(2,1)S(1)}, bf16[1,32,128,64]{2,3,1,0:T(8,128)(2,1)}, u32[]{:S(2)}) %copy-start) | copy-done | bytes 524312
  1.7 0.0 copy-start.1
  1.7 1.0 %copy-done.1 = bf16[1,32,128,64]{2,3,1,0:T(8,128)(2,1)S(1)} copy-done((bf16[1,32,128,64]{2,3,1,0:T(8,128)(2,1)S(1)}, bf16[1,32,128,64]{2,3,1,0:T(8,128)(2,1)}, u32[]{:S(2)}) %copy-start.1) | copy-done | bytes 524312
  2.7 0.0 copy-start.2
  2.7 0.7 copy-done.2
  3.4 71.0 %butterfly.1 = (bf16[4,128,256]{2,1,0:T(8,128)(2,1)S(1)}, bf16[32,128,256]{2,1,0:T(8,128)(2,1)S(1)}) custom-call(bf16[32,128,256]{2,1,0:T(8,128)(2,1)} %bitcast.18, bf16[32,128,256]{2,1,0:T(8,128)(2,1)} %bitcast.19, bf16[32,64,128]{2,1,0:T(8,128)(2,1)S(1)} %bitcast.13, bf16[32,64,128]{2,1,0:T(8,128)(2,1)S(1)} %bitcast.14, ...), custom_call_target="tpu_custom_call" | custom-call | tf_op jit(solution)/shard_map/butterfly/pallas_call | solution.py:297
  74.4 0.7 copy.10
  75.1 1.3 %copy.11 = bf16[1,4096,256]{2,1,0:T(8,128)(2,1)} copy(bf16[1,4096,256]{2,1,0:T(8,128)(2,1)S(1)} %bitcast.12) | data formatting | bytes 4194304
Async XLA Ops:
  0.6 1.0 %copy-start = (bf16[1,32,128,64]{2,3,1,0:T(8,128)(2,1)S(1)}, bf16[1,32,128,64]{2,3,1,0:T(8,128)(2,1)}, u32[]{:S(2)}) copy-start(bf16[1,32,128,64]{2,3,1,0:T(8,128)(2,1)} %param.8) | copy-start | bytes 1572868
  1.7 1.0 %copy-start.1 = (bf16[1,32,128,64]{2,3,1,0:T(8,128)(2,1)S(1)}, bf16[1,32,128,64]{2,3,1,0:T(8,128)(2,1)}, u32[]{:S(2)}) copy-start(bf16[1,32,128,64]{2,3,1,0:T(8,128)(2,1)} %param.9) | copy-start | bytes 1572868
  2.7 0.7 copy-start.2

commit v3 on v2

--- a/solution.py
+++ b/solution.py
@@ -22,12 +22,12 @@
 
 
 def kernel(
-    right_hbm, rows_hbm, basis_in, basis_out, tiles_hbm, ranks,
-    row_out, col_out,
-    right, rows, tiles, turned, ping, pong,
+    right_hbm, rows_hbm, basis_in_hbm, basis_out_hbm, tiles_hbm, ranks_hbm,
+    row_out, adj_out, basis_in,
+    right, rows, basis_out, ranks, tiles, turned, ping, pong, third, fourth,
     send_f, recv_f, send_a, recv_a,
     part, swap, pair_sum, gathered,
-    load_sem, tile_sem,
+    load_sem, basis_sem, tile_sem,
     ssem_f, rsem_f, ssem_a, rsem_a, ssem_c, rsem_c, ssem_y, rsem_y,
 ):
     me = lax.axis_index("lvl")
@@ -50,9 +50,10 @@
     tile_loads = [
         pltpu.make_async_copy(tiles_hbm.at[l], tiles.at[l], tile_sem.at[l]) for l in range(LEVELS)
     ]
-    for copy in loads["right"] + tile_loads[:MIDDLE]:
-        copy.start()
-    for copy in loads["rows"] + tile_loads[: MIDDLE - 1 : -1]:
+    load_ranks = pltpu.make_async_copy(ranks_hbm, ranks, basis_sem.at[0])
+    load_in = pltpu.make_async_copy(basis_in_hbm, basis_in, basis_sem.at[1])
+    load_out = pltpu.make_async_copy(basis_out_hbm, basis_out, basis_sem.at[2])
+    for copy in [load_ranks, load_in] + loads["right"] + tile_loads[:MIDDLE]:
         copy.start()
 
     barrier = pltpu.get_barrier_semaphore()
@@ -132,6 +133,8 @@
 
         lax.fori_loop(max(first, 1), last, step, 0)
 
+    load_ranks.wait()
+    load_in.wait()
     for c in range(4):
         loads["right"][c].wait()
         for n in range(c * quarter, (c + 1) * quarter):
@@ -146,6 +149,8 @@
             put_pair(dst, 2 * t, 2 * t + 1, out, level)
         src, dst = dst, src
     tile_loads[MIDDLE - 1].wait()
+    for copy in [load_out] + loads["rows"] + tile_loads[: MIDDLE - 1 : -1]:
+        copy.start()
     pl.semaphore_wait(barrier, NODES - 1 + CHIPS)
     for part_k in (1, 0):
         for k in range(part_k * 8, part_k * 8 + 8):
@@ -155,6 +160,7 @@
         send(copy_f, 16 * part_k, 16 * part_k + 16)
     recv_f[me] = send_f[me]
 
+    load_out.wait()
     for c in range(4):
         loads["rows"][c].wait()
         for n in range(c * quarter, (c + 1) * quarter):
@@ -174,7 +180,6 @@
             j = jnp.bitwise_xor(my_pair, k)
             out = apply_t(matrix(MIDDLE + 1, j, j + PAIRS), two(src, j, j + PAIRS))
             put_pair(send_a, 2 * j, 2 * j + 1, out)
-        send(copy_a, 16 * part_k, 16 * part_k + 16)
     recv_a[me] = send_a[me]
 
     for level in range(1, MIDDLE + 1):
@@ -196,6 +201,16 @@
             turned[level - 1, t, RANK : RANK + HALF] = w[RANK : RANK + HALF]
             turned[level - 1, t, RANK + HALF :] = keep(level - 1, at + span, w[RANK + HALF :])
 
+    def left(first, last):
+        def step(k, carry):
+            copy_f(peer(k), me).wait_send()
+            return carry
+
+        lax.fori_loop(max(first, 1), last, step, 0)
+
+    left(16, NODES)
+    send(copy_a, 16, NODES)
+
     await_from(copy_f, 0, NODES)
     src, dst = recv_f, ping
     for level in range(MIDDLE + 1, LEVELS + 1):
@@ -246,38 +261,47 @@
 
     lax.fori_loop(1, CHIPS, exchange, 0)
     add_pair(chip)
-
-    for part_k in range(4):
-        if part_k == 3:
-            for k in range(1, CHIPS):
-                y = lax.rem(chip + k, CHIPS)
-                y_copy(y, y).wait_recv()
-            for s in range(SHARE):
-                total = pair_sum[chip, s].astype(F32)
-                for k in range(1, CHIPS):
-                    total = total + gathered[lax.rem(chip + k, CHIPS), s].astype(F32)
-                row_out[s] = total.astype(BF16)
-        group_k = 3 - part_k
-        await_from(copy_a, 8 * group_k, 8 * group_k + 8)
-        for k in range(4 * group_k, 4 * group_k + 4):
-            h = jnp.bitwise_xor(my_pair, k)
-            out = apply(turned[MIDDLE - 1, h], two(recv_a, 2 * h, 2 * h + 1)).astype(BF16)
-            ping[h] = out[:RANK]
-            ping[h + PAIRS] = out[RANK:]
-    src, dst = ping, pong
-    for level in range(MIDDLE - 1, 0, -1):
+    left(0, 16)
+    send(copy_a, 0, 16)
+
+    def low_t(level, first, last):
         span = 2 ** (level - 1)
-        for t in range(PAIRS):
-            at = 2 * (t // span) * span + t % span
-            out = apply(turned[level - 1, t], two(src, 2 * t, 2 * t + 1)).astype(BF16)
-            dst[at] = out[:RANK]
-            dst[at + span] = out[RANK:]
-        src, dst = dst, src
-    for n in range(NODES):
-        col_out[n] = apply_t(basis_in[n], src[n]).astype(BF16)
+        src, dst = steps[MIDDLE - level], steps[MIDDLE + 1 - level]
+        for k in range(first, last):
+            h = jnp.bitwise_xor(my_pair // (PAIRS // span), k)
+            for j in range(PAIRS // span):
+                t = j * span + h
+                out = apply(turned[level - 1, t], two(src, 2 * t, 2 * t + 1)).astype(BF16)
+                at = 2 * j * span + h
+                dst[at] = out[:RANK]
+                dst[at + span] = out[RANK:]
+
+    steps = (recv_a, ping, pong, third, fourth, adj_out)
+    await_from(copy_a, 16, NODES)
+    low_t(5, 8, 16)
+    low_t(4, 4, 8)
+    low_t(3, 2, 4)
+    low_t(2, 1, 2)
+    await_from(copy_a, 8, 16)
+    low_t(5, 4, 8)
+    low_t(4, 2, 4)
+    low_t(3, 1, 2)
+    for k in range(1, CHIPS):
+        y = lax.rem(chip + k, CHIPS)
+        y_copy(y, y).wait_recv()
+    for n in range(SHARE):
+        total = pair_sum[chip, n].astype(F32)
+        for k in range(1, CHIPS):
+            total = total + gathered[lax.rem(chip + k, CHIPS), n].astype(F32)
+        row_out[n] = total.astype(BF16)
+    await_from(copy_a, 0, 8)
+    low_t(5, 0, 4)
+    low_t(4, 0, 2)
+    low_t(3, 0, 1)
+    low_t(2, 0, 1)
+    low_t(1, 0, 1)
 
     def sent(k, carry):
-        copy_f(peer(k), me).wait_send()
         copy_a(peer(k), me).wait_send()
         return carry
 
@@ -288,25 +312,47 @@
         y_copy(lax.rem(chip + k, CHIPS), chip).wait_send()
 
 
+def finish(row, adjoint, basis, row_out, col_out, col_buf, store_sem):
+    stores = [pltpu.make_async_copy(row, row_out, store_sem.at[4])]
+    stores[0].start()
+    quarter = NODES // 4
+    for c in range(4):
+        for n in range(c * quarter, (c + 1) * quarter):
+            out = lax.dot_general(
+                basis[n], adjoint[n], (((0,), (0,)), ((), ())), preferred_element_type=F32
+            )
+            col_buf[n] = out.astype(BF16)
+        part = pl.ds(c * quarter, quarter)
+        stores.append(pltpu.make_async_copy(col_buf.at[part], col_out.at[part], store_sem.at[c]))
+        stores[-1].start()
+    for copy in stores:
+        copy.wait()
+
+
 def body(right_sides, row_vectors, leaf_basis_in, leaf_basis_out, transfers, tile_ranks):
-    hbm = pl.BlockSpec(memory_space=pl.ANY)
+    hbm = pl.BlockSpec(memory_space=pltpu.HBM)
     vmem = pl.BlockSpec(memory_space=pltpu.VMEM)
     nodes = (NODES, RANK, NRHS)
     leaves = (NODES, LEAF, NRHS)
     dma = pltpu.SemaphoreType.DMA
-    row, col = pl.pallas_call(
+    row, adjoint, basis = pl.pallas_call(
         kernel,
         out_shape=(
             jax.ShapeDtypeStruct((SHARE, LEAF, NRHS), BF16),
-            jax.ShapeDtypeStruct(leaves, BF16),
+            jax.ShapeDtypeStruct(nodes, BF16),
+            jax.ShapeDtypeStruct((NODES, RANK, LEAF), BF16),
         ),
-        in_specs=[hbm, hbm, vmem, vmem, hbm, pl.BlockSpec(memory_space=pltpu.SMEM)],
-        out_specs=(vmem, vmem),
+        in_specs=[hbm] * 6,
+        out_specs=(vmem, vmem, vmem),
         scratch_shapes=[
             pltpu.VMEM(leaves, BF16),
             pltpu.VMEM(leaves, BF16),
+            pltpu.VMEM((NODES, RANK, LEAF), BF16),
+            pltpu.SMEM((LEVELS + 1, 1, NODES), jnp.int32),
             pltpu.VMEM((LEVELS, NODES, 2, RANK, RANK), BF16),
             pltpu.VMEM((MIDDLE, PAIRS, 2 * RANK, 2 * RANK), BF16),
+            pltpu.VMEM(nodes, BF16),
+            pltpu.VMEM(nodes, BF16),
             pltpu.VMEM(nodes, BF16),
             pltpu.VMEM(nodes, BF16),
             pltpu.VMEM(nodes, BF16),
@@ -318,6 +364,7 @@
             pltpu.VMEM((CHIPS, SHARE, LEAF, NRHS), BF16),
             pltpu.VMEM((CHIPS, SHARE, LEAF, NRHS), BF16),
             dma((8,)),
+            dma((3,)),
             dma((LEVELS,)),
             dma((NODES,)),
             dma((NODES,)),
@@ -333,13 +380,30 @@
         ),
         name="butterfly",
     )(
-        right_sides.reshape(leaves),
-        row_vectors.reshape(leaves),
-        jnp.swapaxes(leaf_basis_in[0], 1, 2),
-        jnp.swapaxes(leaf_basis_out[0], 1, 2),
-        transfers[0],
-        jnp.swapaxes(tile_ranks, 0, 1),
+        *(
+            pltpu.with_memory_space_constraint(array, pltpu.HBM)
+            for array in (
+                right_sides.reshape(leaves),
+                row_vectors.reshape(leaves),
+                jnp.swapaxes(leaf_basis_in[0], 1, 2),
+                jnp.swapaxes(leaf_basis_out[0], 1, 2),
+                transfers[0],
+                jnp.swapaxes(tile_ranks, 0, 1),
+            )
+        )
     )
+    row, col = pl.pallas_call(
+        finish,
+        out_shape=(
+            jax.ShapeDtypeStruct((SHARE, LEAF, NRHS), BF16),
+            jax.ShapeDtypeStruct(leaves, BF16),
+        ),
+        in_specs=[vmem, vmem, vmem],
+        out_specs=(hbm, hbm),
+        scratch_shapes=[pltpu.VMEM(leaves, BF16), dma((5,))],
+        compiler_params=pltpu.CompilerParams(vmem_limit_bytes=50 << 20),
+        name="leaves_out",
+    )(row, adjoint, basis)
     return row.reshape(SHARE * LEAF, NRHS), col.reshape(1, NODES * LEAF, NRHS)
 
 

time: 77.5 us -> 70 us (0.903); the launches traced: 76.4 us -> 70 us
  local copies, waits for them, and re-layouts: 4.79 us -> 0 us
  Pallas kernels: 71 us -> 69.2 us
    unnamed x8 -> x0, local copies, waits for them, and re-layouts: 4.79 us -> none
    pallas_call x1, Pallas kernels: 71 us -> 67.5 us  [body(): pl.pallas_call(kernel, out_shape=(jax.ShapeDtypeStruct((SHARE, LEAF, NRHS...]
    pallas_call x0 -> x1, Pallas kernels: none -> 1.69 us  [body(): pl.pallas_call(finish, out_shape=(jax.ShapeDtypeStruct((SHARE, LEAF, NRHS...]
where the time goes in v3:
time: 70 us
  Pallas kernels  69.2 us (99%)
  between operations  0.8 us (1%)
    pallas_call x1, Pallas kernels, body(): pl.pallas_call(kernel, out_shape=(jax.ShapeDtypeStruct((SHARE, LEAF, NRHS...  67.5 us
    pallas_call x1, Pallas kernels, body(): pl.pallas_call(finish, out_shape=(jax.ShapeDtypeStruct((SHARE, LEAF, NRHS...  1.69 us

profile of v3, /device:TPU:1, one launch (start us, length us, event | category | flops | bytes accessed | tf_op | source)
XLA Modules:
  0.0 70.0 jit_solution(8705570675702072034)
XLA Ops:
  0.6 67.5 %butterfly.1 = (bf16[4,128,256]{2,1,0:T(8,128)(2,1)S(1)}, bf16[32,64,256]{2,1,0:T(8,128)(2,1)S(1)}, bf16[32,64,128]{2,1,0:T(8,128)(2,1)S(1)}) custom-call(bf16[32,128,256]{2,1,0:T(8,128)(2,1)} %bitcast.13, bf16[32,128,256]{2,1,0:T(8,128)(2,1)} %bitcast.14, bf16[32,64,128]{2,1,0:T(8,128)(2,1)} %bitcast.15, bf16[32,64,128]{2,1,0:T(8,128)(2,1)} %bitcast.16, ...), custom_call_target="tpu_custom_call" | custom-call | tf_op jit(solution)/shard_map/butterfly/pallas_call | solution.py:338
  68.1 1.7 %leaves_out.1 = (bf16[4,128,256]{2,1,0:T(8,128)(2,1)}, bf16[32,128,256]{2,1,0:T(8,128)(2,1)}) custom-call(bf16[4,128,256]{2,1,0:T(8,128)(2,1)S(1)} %get-tuple-element.7.row, bf16[32,64,256]{2,1,0:T(8,128)(2,1)S(1)} %get-tuple-element.8.adjoint, bf16[32,64,128]{2,1,0:T(8,128)(2,1)S(1)} %get-tuple-element.9.basis), custom_call_target="tpu_custom_call" | custom-call | tf_op jit(solution)/shard_map/leaves_out/pallas_call | solution.py:395

commit v4 on v3

--- a/solution.py
+++ b/solution.py
@@ -16,6 +16,8 @@
 GROUPS = 8
 CHIPS = GROUPS // 2
 SHARE = NODES // GROUPS
+FAR = (4, 3, 5, 2)
+NEAR = (6, 1, 7, 0)
 MESH = pl.DeviceIdType.MESH
 F32 = jnp.float32
 BF16 = jnp.bfloat16
@@ -119,12 +121,17 @@
     def peer(k):
         return jnp.bitwise_xor(me, k)
 
-    def send(copy, first, last):
-        def step(k, carry):
-            copy(peer(k), me).start()
-            return carry
-
-        lax.fori_loop(max(first, 1), last, step, 0)
+    def each(shifts, act):
+        for dz in shifts:
+
+            def step(dx, carry, dz=dz):
+                act(lax.rem(me // 4 + dz, 8) * 4 + lax.rem(me + dx, 4))
+                return carry
+
+            lax.fori_loop(0 if dz else 1, 4, step, 0)
+
+    def send(copy, shifts):
+        each(shifts, lambda q: copy(q, me).start())
 
     def await_from(copy, first, last):
         def step(k, carry):
@@ -151,13 +158,11 @@
     tile_loads[MIDDLE - 1].wait()
     for copy in [load_out] + loads["rows"] + tile_loads[: MIDDLE - 1 : -1]:
         copy.start()
+    for h in range(PAIRS):
+        out = apply(matrix(MIDDLE, 2 * h, 2 * h + 1), two(src, h, h + PAIRS))
+        put_pair(send_f, 2 * h, 2 * h + 1, out, MIDDLE)
     pl.semaphore_wait(barrier, NODES - 1 + CHIPS)
-    for part_k in (1, 0):
-        for k in range(part_k * 8, part_k * 8 + 8):
-            h = jnp.bitwise_xor(my_pair, k)
-            out = apply(matrix(MIDDLE, 2 * h, 2 * h + 1), two(src, h, h + PAIRS))
-            put_pair(send_f, 2 * h, 2 * h + 1, out, MIDDLE)
-        send(copy_f, 16 * part_k, 16 * part_k + 16)
+    send(copy_f, FAR + NEAR)
     recv_f[me] = send_f[me]
 
     load_out.wait()
@@ -175,11 +180,9 @@
             put_pair(dst, 2 * u, 2 * u + 1, out, level - 1)
         src, dst = dst, src
     tile_loads[MIDDLE].wait()
-    for part_k in (1, 0):
-        for k in range(part_k * 8, part_k * 8 + 8):
-            j = jnp.bitwise_xor(my_pair, k)
-            out = apply_t(matrix(MIDDLE + 1, j, j + PAIRS), two(src, j, j + PAIRS))
-            put_pair(send_a, 2 * j, 2 * j + 1, out)
+    for j in range(PAIRS):
+        out = apply_t(matrix(MIDDLE + 1, j, j + PAIRS), two(src, j, j + PAIRS))
+        put_pair(send_a, 2 * j, 2 * j + 1, out)
     recv_a[me] = send_a[me]
 
     for level in range(1, MIDDLE + 1):
@@ -201,15 +204,11 @@
             turned[level - 1, t, RANK : RANK + HALF] = w[RANK : RANK + HALF]
             turned[level - 1, t, RANK + HALF :] = keep(level - 1, at + span, w[RANK + HALF :])
 
-    def left(first, last):
-        def step(k, carry):
-            copy_f(peer(k), me).wait_send()
-            return carry
-
-        lax.fori_loop(max(first, 1), last, step, 0)
-
-    left(16, NODES)
-    send(copy_a, 16, NODES)
+    def left(shifts):
+        each(shifts, lambda q: copy_f(q, me).wait_send())
+
+    left(FAR)
+    send(copy_a, FAR)
 
     await_from(copy_f, 0, NODES)
     src, dst = recv_f, ping
@@ -261,8 +260,8 @@
 
     lax.fori_loop(1, CHIPS, exchange, 0)
     add_pair(chip)
-    left(0, 16)
-    send(copy_a, 0, 16)
+    left(NEAR)
+    send(copy_a, NEAR)
 
     def low_t(level, first, last):
         span = 2 ** (level - 1)
@@ -286,6 +285,12 @@
     low_t(5, 4, 8)
     low_t(4, 2, 4)
     low_t(3, 1, 2)
+    await_from(copy_a, 0, 8)
+    low_t(5, 0, 4)
+    low_t(4, 0, 2)
+    low_t(3, 0, 1)
+    low_t(2, 0, 1)
+    low_t(1, 0, 1)
     for k in range(1, CHIPS):
         y = lax.rem(chip + k, CHIPS)
         y_copy(y, y).wait_recv()
@@ -294,12 +299,6 @@
         for k in range(1, CHIPS):
             total = total + gathered[lax.rem(chip + k, CHIPS), n].astype(F32)
         row_out[n] = total.astype(BF16)
-    await_from(copy_a, 0, 8)
-    low_t(5, 0, 4)
-    low_t(4, 0, 2)
-    low_t(3, 0, 1)
-    low_t(2, 0, 1)
-    low_t(1, 0, 1)
 
     def sent(k, carry):
         copy_a(peer(k), me).wait_send()

time: 70 us -> 67.7 us (0.967)
  Pallas kernels: 69.2 us -> 66.8 us
    pallas_call x1, Pallas kernels: 67.5 us -> 65.1 us  [body(): pl.pallas_call(kernel, out_shape=(jax.ShapeDtypeStruct((SHARE, LEAF, NRHS...]
where the time goes in v4:
time: 67.7 us; the launch traced here: 67.6 us
  Pallas kernels  66.8 us (99%)
  between operations  0.8 us (1%)
    pallas_call x1, Pallas kernels, body(): pl.pallas_call(kernel, out_shape=(jax.ShapeDtypeStruct((SHARE, LEAF, NRHS...  65.1 us
    pallas_call x1, Pallas kernels, body(): pl.pallas_call(finish, out_shape=(jax.ShapeDtypeStruct((SHARE, LEAF, NRHS...  1.69 us

profile of v4, /device:TPU:1, one launch (start us, length us, event | category | flops | bytes accessed | tf_op | source)
XLA Modules:
  0.0 67.6 jit_solution(3570198342013972720)
XLA Ops:
  0.6 65.1 %butterfly.1 = (bf16[4,128,256]{2,1,0:T(8,128)(2,1)S(1)}, bf16[32,64,256]{2,1,0:T(8,128)(2,1)S(1)}, bf16[32,64,128]{2,1,0:T(8,128)(2,1)S(1)}) custom-call(bf16[32,128,256]{2,1,0:T(8,128)(2,1)} %bitcast.13, bf16[32,128,256]{2,1,0:T(8,128)(2,1)} %bitcast.14, bf16[32,64,128]{2,1,0:T(8,128)(2,1)} %bitcast.15, bf16[32,64,128]{2,1,0:T(8,128)(2,1)} %bitcast.16, ...), custom_call_target="tpu_custom_call" | custom-call | tf_op jit(solution)/shard_map/butterfly/pallas_call | solution.py:337
  65.7 1.7 %leaves_out.1 = (bf16[4,128,256]{2,1,0:T(8,128)(2,1)}, bf16[32,128,256]{2,1,0:T(8,128)(2,1)}) custom-call(bf16[4,128,256]{2,1,0:T(8,128)(2,1)S(1)} %get-tuple-element.7.row, bf16[32,64,256]{2,1,0:T(8,128)(2,1)S(1)} %get-tuple-element.8.adjoint, bf16[32,64,128]{2,1,0:T(8,128)(2,1)S(1)} %get-tuple-element.9.basis), custom_call_target="tpu_custom_call" | custom-call | tf_op jit(solution)/shard_map/leaves_out/pallas_call | solution.py:394

commit v5 on v4

--- a/solution.py
+++ b/solution.py
@@ -60,13 +60,14 @@
 
     barrier = pltpu.get_barrier_semaphore()
 
-    def greet(k, carry):
-        pl.semaphore_signal(
-            barrier, inc=1, device_id=(lax.rem(me + k, NODES), blk), device_id_type=MESH
-        )
-        return carry
-
-    lax.fori_loop(1, NODES, greet, 0)
+    for dz in FAR + NEAR:
+
+        def greet(dx, carry, dz=dz):
+            peer_z = lax.rem(me // 4 + dz, 8) * 4 + lax.rem(me + dx, 4)
+            pl.semaphore_signal(barrier, inc=1, device_id=(peer_z, blk), device_id_type=MESH)
+            return carry
+
+        lax.fori_loop(0 if dz else 1, 4, greet, 0)
     for k in range(1, CHIPS):
         other = lax.rem(chip + k, CHIPS) * 2 + core
         pl.semaphore_signal(barrier, inc=1, device_id=(me, other), device_id_type=MESH)

time: 67.7 us -> 67.6 us (level)
  no operation moved by 1% of the time
where the time goes in v5:
time: 67.6 us; the launch traced here: 67.5 us
  Pallas kernels  66.7 us (99%)
  between operations  0.8 us (1%)
    pallas_call x1, Pallas kernels, body(): pl.pallas_call(kernel, out_shape=(jax.ShapeDtypeStruct((SHARE, LEAF, NRHS...  65 us
    pallas_call x1, Pallas kernels, body(): pl.pallas_call(finish, out_shape=(jax.ShapeDtypeStruct((SHARE, LEAF, NRHS...  1.69 us

profile of v5, /device:TPU:1, one launch (start us, length us, event | category | flops | bytes accessed | tf_op | source)
XLA Modules:
  0.0 67.5 jit_solution(15969017903119920561)
XLA Ops:
  0.6 65.0 %butterfly.1 = (bf16[4,128,256]{2,1,0:T(8,128)(2,1)S(1)}, bf16[32,64,256]{2,1,0:T(8,128)(2,1)S(1)}, bf16[32,64,128]{2,1,0:T(8,128)(2,1)S(1)}) custom-call(bf16[32,128,256]{2,1,0:T(8,128)(2,1)} %bitcast.13, bf16[32,128,256]{2,1,0:T(8,128)(2,1)} %bitcast.14, bf16[32,64,128]{2,1,0:T(8,128)(2,1)} %bitcast.15, bf16[32,64,128]{2,1,0:T(8,128)(2,1)} %bitcast.16, ...), custom_call_target="tpu_custom_call" | custom-call | tf_op jit(solution)/shard_map/butterfly/pallas_call | solution.py:338
  65.7 1.7 %leaves_out.1 = (bf16[4,128,256]{2,1,0:T(8,128)(2,1)}, bf16[32,128,256]{2,1,0:T(8,128)(2,1)}) custom-call(bf16[4,128,256]{2,1,0:T(8,128)(2,1)S(1)} %get-tuple-element.7.row, bf16[32,64,256]{2,1,0:T(8,128)(2,1)S(1)} %get-tuple-element.8.adjoint, bf16[32,64,128]{2,1,0:T(8,128)(2,1)S(1)} %get-tuple-element.9.basis), custom_call_target="tpu_custom_call" | custom-call | tf_op jit(solution)/shard_map/leaves_out/pallas_call | solution.py:395
